TPU v7x, 32 devices: a whole 2x2x4 slice. The times are simulated.
32 devices in a mesh: dp: 16 (over z, y, core), tensor: 2 (over x).
Axes of the slice: x: 2, y: 2, z: 4, core: 2. Of those that a mesh axis runs over, the one named last changes fastest.
Arguments:
- tokens: bfloat16 [18432, 1024], P(('dp', 'tensor')), may hold values from -6 to 6
- cotangent: bfloat16 [18432, 1024], P(('dp', 'tensor')), may hold values from -6 to 6
- lengths: int32 [16, 3], P('dp'), may hold values from 1 to 1024, 1152 in all within a row
- qkv_weight: float32 [1024, 3, 1024], P('dp', None, 'tensor'), may hold values from -0.1875 to 0.1875
- proj_weight: float32 [1024, 1024], P('tensor', 'dp'), may hold values from -1.5 to 1.5
- up_weight: float32 [1024, 4096], P('dp', 'tensor'), may hold values from -0.1875 to 0.1875
- down_weight: float32 [4096, 1024], P('tensor', 'dp'), may hold values from -0.09375 to 0.09375
- small_params: float32 [13, 1024], P(None, ('dp', 'tensor')), may hold values from -1.2 to 1.4
- qkv_first: float32 [1024, 3, 1024], P('dp', None, 'tensor'), may hold values from -48 to 48
- proj_first: float32 [1024, 1024], P('tensor', 'dp'), may hold values from -8 to 8
- up_first: float32 [1024, 4096], P('dp', 'tensor'), may hold values from -28 to 28
- down_first: float32 [4096, 1024], P('tensor', 'dp'), may hold values from -64 to 64
- small_first: float32 [13, 1024], P(None, ('dp', 'tensor')), may hold values from -96 to 96
- qkv_second: float32 [1024, 3, 1024], P('dp', None, 'tensor'), may hold values from 258.048 to 1013.76
- proj_second: float32 [1024, 1024], P('tensor', 'dp'), may hold values from 10.1376 to 40.5504
- up_second: float32 [1024, 4096], P('dp', 'tensor'), may hold values from 92.16 to 368.64
- down_second: float32 [4096, 1024], P('tensor', 'dp'), may hold values from 497.664 to 1990.656
- small_second: float32 [13, 1024], P(None, ('dp', 'tensor')), may hold values from 1013.76 to 4055.04
Outputs:
- block_out: bfloat16 [18432, 1024], P(('dp', 'tensor'))
- token_grad: float32 [18432, 1024], P(('dp', 'tensor'))
- qkv_first_new: float32 [1024, 3, 1024], P('dp', None, 'tensor')
- qkv_second_new: float32 [1024, 3, 1024], P('dp', None, 'tensor')
- qkv_weight_new: float32 [1024, 3, 1024], P('dp', None, 'tensor')
- proj_first_new: float32 [1024, 1024], P('tensor', 'dp')
- proj_second_new: float32 [1024, 1024], P('tensor', 'dp')
- proj_weight_new: float32 [1024, 1024], P('tensor', 'dp')
- up_first_new: float32 [1024, 4096], P('dp', 'tensor')
- up_second_new: float32 [1024, 4096], P('dp', 'tensor')
- up_weight_new: float32 [1024, 4096], P('dp', 'tensor')
- down_first_new: float32 [4096, 1024], P('tensor', 'dp')
- down_second_new: float32 [4096, 1024], P('tensor', 'dp')
- down_weight_new: float32 [4096, 1024], P('tensor', 'dp')
- small_first_new: float32 [13, 1024], P(None, ('dp', 'tensor'))
- small_second_new: float32 [13, 1024], P(None, ('dp', 'tensor'))
- small_params_new: float32 [13, 1024], P(None, ('dp', 'tensor'))
Inputs may be any that keep to these rules, and one draw needn't show every extreme that they name: `lengths`: each row sums to 1152 and its largest entry is exactly 1024.
All inputs are finite; a program needn't handle non-finite values.
Results may differ from a plain program's by a relative error of at most 0.02.
Values may be sent and summed in bfloat16 or wider, within the bound.
No kernel may reach another device: no remote copies, remote signals or barrier semaphores. Data moves between devices by JAX's collectives and lax.ppermute only.
A program may use at most 192 MiB of HBM per device.

v0:
```python
import math

import jax
import jax.numpy as jnp
from jax import lax
from jax.sharding import PartitionSpec as P

D = 1024
HD = 64
FF = 4096
ROT = 16
STEP = 10


EPS_NORM = 1e-05
BETA_ONE = 0.9
BETA_TWO = 0.95
EPS_ADAM = 1e-08
DECAY = 0.01
SMALL_RATE = 0.3
BFLOAT = jnp.bfloat16
FLOAT = jnp.float32
ROOT_HALF = 1.0 / math.sqrt(2.0)
INV_ROOT_TAU = 1.0 / math.sqrt(2.0 * math.pi)


def layout(lengths_row, row_count):
    starts = jnp.cumsum(lengths_row) - lengths_row
    row_index = jnp.arange(row_count, dtype=jnp.int32)
    member = (row_index[:, None] >= starts[None, :]).astype(jnp.int32)
    sequence = jnp.sum(member, axis=1) - 1
    onehot = (
        sequence[:, None] == jnp.arange(lengths_row.shape[0], dtype=jnp.int32)[None, :]
    ).astype(jnp.int32)
    position = row_index - jnp.sum(onehot * starts[None, :], axis=1)
    return (sequence, position)


def rotary_tables(position, rot_dims):
    half_rot = rot_dims // 2
    frequency = 10000.0 ** (-(2.0 * jnp.arange(half_rot, dtype=FLOAT)) / rot_dims)
    angles = position.astype(FLOAT)[:, None] * frequency[None, :]
    angles = jnp.concatenate([angles, angles], axis=1)
    return (jnp.cos(angles), jnp.sin(angles))


def rotate(tensor, cosine, sine_table):
    rot_dims = cosine.shape[1]
    half_rot = rot_dims // 2
    rotated = tensor[..., :rot_dims]
    turned = jnp.concatenate([-rotated[..., half_rot:], rotated[..., :half_rot]], axis=-1)
    rotated = rotated * cosine[:, None, :] + turned * sine_table[:, None, :]
    return jnp.concatenate([rotated, tensor[..., rot_dims:]], axis=-1)


def unrotate(tensor, cosine, sine_table):
    rot_dims = cosine.shape[1]
    half_rot = rot_dims // 2
    scaled_result = tensor[..., :rot_dims] * sine_table[:, None, :]
    turned = jnp.concatenate(
        [scaled_result[..., half_rot:], -scaled_result[..., :half_rot]], axis=-1
    )
    rotated = tensor[..., :rot_dims] * cosine[:, None, :] + turned
    return jnp.concatenate([rotated, tensor[..., rot_dims:]], axis=-1)


def apply_layer_norm(layer_inputs):
    average = jnp.mean(layer_inputs, axis=-1, keepdims=True)
    centred = layer_inputs - average
    variance = jnp.mean(centred * centred, axis=-1, keepdims=True)
    inverse_deviation = lax.rsqrt(variance + EPS_NORM)
    return (centred * inverse_deviation, inverse_deviation)


def norm_backward_pass(gradient_norm_total, centered_whitened, inverse_deviation, norm_gain_vector):
    scaled_result = gradient_norm_total * norm_gain_vector
    first_moment_mean = jnp.mean(scaled_result, axis=-1, keepdims=True)
    second_moment_mean = jnp.mean(scaled_result * centered_whitened, axis=-1, keepdims=True)
    return inverse_deviation * (
        scaled_result - first_moment_mean - centered_whitened * second_moment_mean
    )


def norm_partial_sums(gradient_attention_norm, gradient_feedforward_norm, centered_whitened):
    return jnp.stack(
        [
            jnp.sum(gradient_attention_norm * centered_whitened, axis=0),
            jnp.sum(gradient_attention_norm, axis=0),
            jnp.sum(gradient_feedforward_norm * centered_whitened, axis=0),
            jnp.sum(gradient_feedforward_norm, axis=0),
        ]
    )


def adamw(weight, moment, second, gradient, step_rate, decay_rate):
    moment = BETA_ONE * moment + (1.0 - BETA_ONE) * gradient
    second = BETA_TWO * second + (1.0 - BETA_TWO) * gradient * gradient
    moment_hat = moment / (1.0 - BETA_ONE**STEP)
    second_hat = second / (1.0 - BETA_TWO**STEP)
    weight = weight - step_rate * (
        moment_hat / (jnp.sqrt(second_hat) + EPS_ADAM) + decay_rate * weight
    )
    return (moment, second, weight)


def per_device(
    tokens,
    cotangent,
    lengths,
    qkv_weight,
    proj_weight,
    up_weight,
    down_weight,
    small_params,
    qkv_first,
    proj_first,
    up_first,
    down_first,
    small_first,
    qkv_second,
    proj_second,
    up_second,
    down_second,
    small_second,
):
    tensor_rank = lax.axis_index("tensor")
    local_width = qkv_weight.shape[2]
    hidden_width = up_weight.shape[1]
    heads_here = local_width // HD
    shards = (
        qkv_weight.astype(BFLOAT),
        proj_weight.astype(BFLOAT),
        up_weight.astype(BFLOAT),
        down_weight.astype(BFLOAT),
    )
    qkv_full, proj_full, up_full, down_full = (
        lax.all_gather(shards[0], "dp", axis=0, tiled=True),
        lax.all_gather(shards[1], "dp", axis=1, tiled=True),
        lax.all_gather(shards[2], "dp", axis=0, tiled=True),
        lax.all_gather(shards[3], "dp", axis=1, tiled=True),
    )
    small_parameters = lax.all_gather(small_params, ("dp", "tensor"), axis=1, tiled=True)
    model_width = small_parameters.shape[1]
    bias_qkv = lax.dynamic_slice_in_dim(
        small_parameters[4:7], tensor_rank * local_width, local_width, 1
    )
    bias_up = lax.dynamic_slice_in_dim(
        small_parameters[8:12].reshape(4 * model_width), tensor_rank * hidden_width, hidden_width, 0
    )
    own_inputs = tokens.astype(FLOAT)
    own_hat, own_inv = apply_layer_norm(own_inputs)
    own_a = (own_hat * small_parameters[0] + small_parameters[1]).astype(BFLOAT)
    own_m = (own_hat * small_parameters[2] + small_parameters[3]).astype(BFLOAT)
    attention_normed_rows, feedforward_normed_rows, grad_rows = (
        lax.all_gather(own_a, "tensor", axis=0, tiled=True),
        lax.all_gather(own_m, "tensor", axis=0, tiled=True),
        lax.all_gather(cotangent, "tensor", axis=0, tiled=True),
    )
    row_count = attention_normed_rows.shape[0]
    sequence, position = layout(lengths[0], row_count)
    cosine, sine_table = rotary_tables(position, ROT)
    row_index = jnp.arange(row_count, dtype=jnp.int32)
    blocks = max(1, row_count // 576)
    block_rows = row_count // blocks
    scale = HD ** (-0.5)

    def to_items(tensor):
        return tensor.transpose(1, 0, 2).reshape(heads_here * blocks, block_rows, HD)

    def from_items(tensor):
        return tensor.reshape(heads_here, row_count, HD).transpose(1, 0, 2)

    def spread(tensor):
        return jnp.repeat(tensor.transpose(1, 0, 2), blocks, axis=0)

    def fold_keys(tensor):
        return jnp.sum(tensor.reshape(heads_here, blocks, row_count, HD), axis=1).transpose(1, 0, 2)

    seq_items = jnp.tile(sequence.reshape(blocks, block_rows), (heads_here, 1))
    idx_items = jnp.tile(row_index.reshape(blocks, block_rows), (heads_here, 1))

    def masked_scores(query_blk, key_all, seq_q, idx_q):
        scores = jnp.einsum("qd,kd->qk", query_blk, key_all, preferred_element_type=FLOAT) * scale
        allowed = (seq_q[:, None] == sequence[None, :]) & (row_index[None, :] <= idx_q[:, None])
        return jnp.where(allowed, scores, -1e30)

    def attend(pieces):
        query_blk, key_all, value_all, seq_q, idx_q = pieces
        scores = masked_scores(query_blk, key_all, seq_q, idx_q)
        top = jnp.max(scores, axis=-1, keepdims=True)
        expo = jnp.exp(scores - top)
        total = jnp.sum(expo, axis=-1, keepdims=True)
        probs = (expo / total).astype(BFLOAT)
        out_blk = jnp.dot(probs, value_all, preferred_element_type=FLOAT)
        return (out_blk, (top + jnp.log(total))[:, 0])

    def attend_back(pieces):
        query_blk, key_all, value_all, seq_q, idx_q, grad_blk, logsum = pieces
        scores = masked_scores(query_blk, key_all, seq_q, idx_q)
        probs = jnp.exp(scores - logsum[:, None])
        dprob = jnp.einsum("qd,kd->qk", grad_blk, value_all, preferred_element_type=FLOAT)
        delta = jnp.sum(dprob * probs, axis=-1, keepdims=True)
        dscore = (probs * (dprob - delta)).astype(BFLOAT)
        dquery = jnp.dot(dscore, key_all, preferred_element_type=FLOAT) * scale
        dkey = jnp.einsum("qk,qd->kd", dscore, query_blk, preferred_element_type=FLOAT) * scale
        dvalue = jnp.einsum(
            "qk,qd->kd", probs.astype(BFLOAT), grad_blk, preferred_element_type=FLOAT
        )
        return (dquery, dkey, dvalue)

    qkv_pre = (
        jnp.einsum("td,dce->tce", attention_normed_rows, qkv_full, preferred_element_type=FLOAT)
        + bias_qkv[None]
    )
    split = qkv_pre.reshape(row_count, 3, heads_here, HD)
    queries = rotate(split[:, 0], cosine, sine_table).astype(BFLOAT)
    key_rows = rotate(split[:, 1], cosine, sine_table).astype(BFLOAT)
    value_rows = split[:, 2].astype(BFLOAT)
    query_items = to_items(queries)
    key_items = spread(key_rows)
    value_items = spread(value_rows)
    out_items, logsum = lax.map(attend, (query_items, key_items, value_items, seq_items, idx_items))
    attended = from_items(out_items).reshape(row_count, local_width).astype(BFLOAT)
    hidden_pre = jnp.dot(feedforward_normed_rows, up_full, preferred_element_type=FLOAT) + bias_up
    hidden = jax.nn.gelu(hidden_pre, approximate=False).astype(BFLOAT)
    summed = lax.psum_scatter(
        (
            jnp.dot(attended, proj_full, preferred_element_type=FLOAT)
            + jnp.dot(hidden, down_full, preferred_element_type=FLOAT)
        ).astype(jnp.bfloat16),
        "tensor",
        scatter_dimension=0,
        tiled=True,
    ).astype(jnp.float32)
    block_out = (own_inputs + summed + small_parameters[7] + small_parameters[12]).astype(BFLOAT)
    regathered = (
        lax.all_gather(shards[0], "dp", axis=0, tiled=True),
        lax.all_gather(shards[1], "dp", axis=1, tiled=True),
        lax.all_gather(shards[2], "dp", axis=0, tiled=True),
        lax.all_gather(shards[3], "dp", axis=1, tiled=True),
    )
    qkv_back, proj_back, up_back, down_back = regathered
    d_attended = jnp.einsum("td,ed->te", grad_rows, proj_back, preferred_element_type=FLOAT).astype(
        BFLOAT
    )
    proj_grad = jnp.einsum("te,td->ed", attended, grad_rows, preferred_element_type=FLOAT)
    down_grad = jnp.einsum("tf,td->fd", hidden, grad_rows, preferred_element_type=FLOAT)
    d_hidden = jnp.einsum("td,fd->tf", grad_rows, down_back, preferred_element_type=FLOAT)
    normal_cdf = 0.5 * (1.0 + lax.erf(hidden_pre * ROOT_HALF))
    density = jnp.exp(-0.5 * hidden_pre * hidden_pre) * INV_ROOT_TAU
    d_pre = (d_hidden * (normal_cdf + hidden_pre * density)).astype(BFLOAT)
    up_grad = jnp.einsum("td,tf->df", feedforward_normed_rows, d_pre, preferred_element_type=FLOAT)
    up_bias_grad = jnp.sum(d_pre, axis=0, dtype=FLOAT)
    d_normed_m = jnp.einsum("tf,df->td", d_pre, up_back, preferred_element_type=FLOAT)
    grad_items = to_items(d_attended.reshape(row_count, heads_here, HD))
    dq_items, dk_items, dv_items = lax.map(
        attend_back, (query_items, key_items, value_items, seq_items, idx_items, grad_items, logsum)
    )
    dquery = unrotate(from_items(dq_items), cosine, sine_table)
    dkey = unrotate(fold_keys(dk_items), cosine, sine_table)
    dvalue = fold_keys(dv_items)
    d_qkv = (
        jnp.stack([dquery, dkey, dvalue], axis=1).reshape(row_count, 3, local_width).astype(BFLOAT)
    )
    qkv_grad = jnp.einsum("td,tce->dce", attention_normed_rows, d_qkv, preferred_element_type=FLOAT)
    qkv_bias_grad = jnp.sum(d_qkv, axis=0, dtype=FLOAT)
    d_normed_a = jnp.einsum("tce,dce->td", d_qkv, qkv_back, preferred_element_type=FLOAT)
    d_a_own, d_m_own = (
        lax.psum_scatter(
            d_normed_a.astype(jnp.bfloat16), "tensor", scatter_dimension=0, tiled=True
        ).astype(jnp.float32),
        lax.psum_scatter(
            d_normed_m.astype(jnp.bfloat16), "tensor", scatter_dimension=0, tiled=True
        ).astype(jnp.float32),
    )
    token_grad = (
        cotangent.astype(FLOAT)
        + norm_backward_pass(d_a_own, own_hat, own_inv, small_parameters[0])
        + norm_backward_pass(d_m_own, own_hat, own_inv, small_parameters[2])
    )
    norm_rows = norm_partial_sums(d_a_own, d_m_own, own_hat)
    out_bias_grad = jnp.sum(cotangent, axis=0, dtype=FLOAT)
    qkv_rows = lax.dynamic_update_slice_in_dim(
        jnp.zeros((3, model_width), FLOAT), qkv_bias_grad, tensor_rank * local_width, 1
    )
    up_rows = lax.dynamic_update_slice_in_dim(
        jnp.zeros((4 * model_width,), FLOAT), up_bias_grad, tensor_rank * hidden_width, 0
    )
    small_local = jnp.concatenate(
        [
            norm_rows,
            qkv_rows,
            out_bias_grad[None],
            up_rows.reshape(4, model_width),
            out_bias_grad[None],
        ],
        axis=0,
    )
    small_grad = lax.psum_scatter(small_local, ("dp", "tensor"), scatter_dimension=1, tiled=True)
    qkv_owned, proj_owned, up_owned, down_owned = (
        lax.psum_scatter(
            qkv_grad.astype(jnp.bfloat16), "dp", scatter_dimension=0, tiled=True
        ).astype(jnp.float32),
        lax.psum_scatter(
            proj_grad.astype(jnp.bfloat16), "dp", scatter_dimension=1, tiled=True
        ).astype(jnp.float32),
        lax.psum_scatter(
            up_grad.astype(jnp.bfloat16), "dp", scatter_dimension=0, tiled=True
        ).astype(jnp.float32),
        lax.psum_scatter(
            down_grad.astype(jnp.bfloat16), "dp", scatter_dimension=1, tiled=True
        ).astype(jnp.float32),
    )
    qkv_new = adamw(qkv_weight, qkv_first, qkv_second, qkv_owned, D ** (-0.5), DECAY)
    proj_new = adamw(proj_weight, proj_first, proj_second, proj_owned, (D // 64) ** (-0.5), DECAY)
    up_new = adamw(up_weight, up_first, up_second, up_owned, D ** (-0.5), DECAY)
    down_new = adamw(down_weight, down_first, down_second, down_owned, FF ** (-0.5), DECAY)
    small_new = adamw(small_params, small_first, small_second, small_grad, SMALL_RATE, 0.0)
    return (
        block_out,
        token_grad,
        qkv_new[0],
        qkv_new[1],
        qkv_new[2],
        proj_new[0],
        proj_new[1],
        proj_new[2],
        up_new[0],
        up_new[1],
        up_new[2],
        down_new[0],
        down_new[1],
        down_new[2],
        small_new[0],
        small_new[1],
        small_new[2],
    )


def solution(mesh):
    return jax.shard_map(
        per_device,
        mesh=mesh,
        in_specs=(
            P(("dp", "tensor"), None),
            P(("dp", "tensor"), None),
            P("dp", None),
            P("dp", None, "tensor"),
            P("tensor", "dp"),
            P("dp", "tensor"),
            P("tensor", "dp"),
            P(None, ("dp", "tensor")),
            P("dp", None, "tensor"),
            P("tensor", "dp"),
            P("dp", "tensor"),
            P("tensor", "dp"),
            P(None, ("dp", "tensor")),
            P("dp", None, "tensor"),
            P("tensor", "dp"),
            P("dp", "tensor"),
            P("tensor", "dp"),
            P(None, ("dp", "tensor")),
        ),
        out_specs=(
            P(("dp", "tensor"), None),
            P(("dp", "tensor"), None),
            P("dp", None, "tensor"),
            P("dp", None, "tensor"),
            P("dp", None, "tensor"),
            P("tensor", "dp"),
            P("tensor", "dp"),
            P("tensor", "dp"),
            P("dp", "tensor"),
            P("dp", "tensor"),
            P("dp", "tensor"),
            P("tensor", "dp"),
            P("tensor", "dp"),
            P("tensor", "dp"),
            P(None, ("dp", "tensor")),
            P(None, ("dp", "tensor")),
            P(None, ("dp", "tensor")),
        ),
        check_vma=False,
    )
```

profile of v0, /device:TPU:0, one launch (start us, length us, event | category | flops | bytes accessed | tf_op | source)
XLA Modules:
  0.0 1244.5 jit_solution(16576339625743587395)
XLA Ops:
  7.2 71.4 %all-gather = f32[32,32,13]{1,2,0:T(8,128)S(1)} all-gather(f32[1,32,13]{1,2,0:T(8,128)} %bitcast.209), channel_id=1, replica_groups=mesh['dp'=16,'tensor'=2] {'dp','tensor'}, dimensions={0}, use_global_device_ids=true | all-gather | bytes 54912 | tf_op jit(solution)/shard_map/all_gather | solution.py:142
  87.4 28.4 %all-gather.9.cloned.1.call-done = bf16[1152,1024]{1,0:T(8,128)(2,1)} async-done(((bf16[576,1024]{1,0:T(8,128)(2,1)}), bf16[1152,1024]{1,0:T(8,128)(2,1)}) %all-gather.9.cloned.1.call-update) | async-done | bytes 2359312 | tf_op jit(solution)/shard_map/all_gather | solution.py:155
  115.8 48.0 %all-gather.11.cloned.1.call-done = bf16[1024,3,512]{2,0,1:T(8,128)(2,1)} async-done(((bf16[64,3,512]{2,0,1:T(8,128)(2,1)}), bf16[1024,3,512]{2,0,1:T(8,128)(2,1)}) %all-gather.11.cloned.1.call-update) | async-done | bytes 3145744 | tf_op jit(solution)/shard_map/all_gather | solution.py:137
  163.8 7.2 convolution_add_fusion.1
  192.7 112.0 %while.28 = (s32[]{:T(128)}, bf16[16,576,64]{1,2,0:T(8,128)(2,1)}, f32[16,576]{1,0:T(8,128)}, s32[16,576]{1,0:T(8,128)}, s32[1152]{0:T(1024)S(1)}, /*index=5*/s3...) while((s32[]{:T(128)}, bf16[16,576,64]{1,2,0:T(8,128)(2,1)}, ...), condition=%wide.region_8.9_spmd.clone, body=%wide.region_5.8_spmd.clone.sunk | while | flops 177167808 | bytes 8911989 | solution.py:222
  314.8 54.2 %reduce-scatter.19.cloned.1.call-done = bf16[512,64]{0,1:T(8,128)(2,1)} async-done(((bf16[512,1024]{0,1:T(8,128)(2,1)}), bf16[512,64]{0,1:T(8,128)(2,1)}) %reduce-scatter.19.cloned.1.call-update) | async-done | bytes 65552 | tf_op jit(solution)/shard_map/reduce_scatter | solution.py:304
  370.7 34.8 %all-gather.15.cloned.1.call-done = bf16[1152,1024]{1,0:T(8,128)(2,1)} async-done(((bf16[576,1024]{1,0:T(8,128)(2,1)}), bf16[1152,1024]{1,0:T(8,128)(2,1)}) %all-gather.15.cloned.1.call-update) | async-done | bytes 2359312 | tf_op jit(solution)/shard_map/all_gather | solution.py:156
  405.6 53.4 %all-gather.17.cloned.1.call-done = bf16[1024,2048]{1,0:T(8,128)(2,1)} async-done(((bf16[64,2048]{1,0:T(8,128)(2,1)}), bf16[1024,2048]{1,0:T(8,128)(2,1)}) %all-gather.17.cloned.1.call-update) | async-done | bytes 4194320 | tf_op jit(solution)/shard_map/all_gather | solution.py:139
  459.0 28.4 %fusion.49 = (bf16[1152,2048]{1,0:T(8,128)(2,1)S(1)}, f32[1152,2048]{1,0:T(8,128)}) fusion(f32[2048]{0:T(1024)S(1)} %dynamic_slice.47, bf16[1152,1024]{1,0:T(8,128)(2,1)} %all-gather.15.cloned.1.call-done, bf16[1024,2048]{1,0:T(8,128)(2,1)} %all-gather.17.cloned.1.call-done), kind=kOutput, calls=%fused_computation.67 | convolution fusion | flops 4987551744 | bytes 20717568 | tf_op jit(solution)/shard_map/dot_general | solution.py:224
  489.6 8.9 convolution_convert_fusion
  505.4 68.7 %reduce-scatter.23.cloned.1.call-done = bf16[2048,64]{0,1:T(8,128)(2,1)} async-done(((bf16[2048,1024]{0,1:T(8,128)(2,1)}), bf16[2048,64]{0,1:T(8,128)(2,1)}) %reduce-scatter.23.cloned.1.call-update) | async-done | bytes 262160 | tf_op jit(solution)/shard_map/reduce_scatter | solution.py:310
  576.7 250.3 %while.29 = (s32[]{:T(128)}, f32[16,576,64]{1,0,2:T(8,128)}, f32[16,1152,64]{1,2,0:T(8,128)}, f32[16,1152,64]{1,2,0:T(8,128)}, s32[16,576]{1,0:T(8,128)}, /*inde...) while((s32[]{:T(128)}, f32[16,576,64]{1,0,2:T(8,128)}, ...), condition=%wide.region_12.13_spmd.clone, body=%wide.region_10.12_spmd.clone.sunk | while | flops 432745920 | bytes 22742928 | solution.py:256
  841.1 7.4 bitcast_convert_fusion
  848.6 12.1 convert_reduce_fusion
  862.9 6.4 convolution_convert_fusion.2
  869.3 8.4 fusion.129
  880.9 8.0 fusion.95
  891.7 28.3 %reduce-scatter.15.cloned.1.call-done = bf16[576,1024]{1,0:T(8,128)(2,1)} async-done(((bf16[1152,1024]{1,0:T(8,128)(2,1)}), bf16[576,1024]{1,0:T(8,128)(2,1)}) %reduce-scatter.15.cloned.1.call-update) | async-done | bytes 1179664 | tf_op jit(solution)/shard_map/reduce_scatter | solution.py:272
  926.7 30.2 %reduce-scatter.11.cloned.1.call-done = bf16[576,1024]{1,0:T(8,128)(2,1)} async-done(((bf16[1152,1024]{1,0:T(8,128)(2,1)}), bf16[576,1024]{1,0:T(8,128)(2,1)}) %reduce-scatter.11.cloned.1.call-update) | async-done | bytes 1179664 | tf_op jit(solution)/shard_map/reduce_scatter | solution.py:226
  956.9 5.2 convert_reduce_fusion.5
  964.8 9.8 convolution_convert_fusion.1
  974.7 52.6 %reduce-scatter.17.cloned.1.call-done = bf16[64,3,512]{2,0,1:T(8,128)(2,1)} async-done(((bf16[1024,3,512]{2,0,1:T(8,128)(2,1)}), bf16[64,3,512]{2,0,1:T(8,128)(2,1)}) %reduce-scatter.17.cloned.1.call-update) | async-done | bytes 196624 | tf_op jit(solution)/shard_map/reduce_scatter | solution.py:301
  1029.5 133.6 %reduce-scatter.25.cloned.1.call-done = f32[32,13]{1,0:T(8,128)} async-done(((f32[1024,13]{1,0:T(8,128)}), f32[32,13]{1,0:T(8,128)}) %reduce-scatter.25.cloned.1.call-update) | async-done | bytes 1680
  1164.4 71.0 %reduce-scatter.21.cloned.1.call-done = bf16[64,2048]{1,0:T(8,128)(2,1)} async-done(((bf16[1024,2048]{1,0:T(8,128)(2,1)}), bf16[64,2048]{1,0:T(8,128)(2,1)}) %reduce-scatter.21.cloned.1.call-update) | async-done | bytes 262160 | tf_op jit(solution)/shard_map/reduce_scatter | solution.py:307
  (489 shorter events, 452.1 us)
Async XLA Ops:
  7.2 73.8 %copy-start = (bf16[576,1024]{1,0:T(8,128)(2,1)S(1)}, bf16[576,1024]{1,0:T(8,128)(2,1)}, u32[]{:S(2)}) copy-start(bf16[576,1024]{1,0:T(8,128)(2,1)} %param.22) | copy-start | bytes 3538948
  7.2 108.6 %all-gather.9.cloned.1.call-start = ((), (), s32[]{:S(2)}) async-start(), calls=%async_computation.8 | async-start | bytes 3538944 | tf_op jit(solution)/shard_map/all_gather | solution.py:155
  83.7 80.1 %all-gather.11.cloned.1.call-start = ((), (), s32[]{:S(2)}) async-start(), calls=%async_computation.9 | async-start | bytes 3342336 | tf_op jit(solution)/shard_map/all_gather | solution.py:137
  84.5 223.4 %all-gather.21.cloned.1.call-start = ((), (), s32[]{:S(2)}) async-start(), calls=%async_computation.15 | async-start | bytes 3538944 | tf_op jit(solution)/shard_map/all_gather | solution.py:157
  85.2 283.8 %reduce-scatter.19.cloned.1.call-start = ((), (), s32[]{:S(2)}) async-start(), calls=%async_computation.19 | async-start | bytes 1114112 | tf_op jit(solution)/shard_map/reduce_scatter | solution.py:304
  86.0 86.7 %copy-start.14 = (f32[1152,16]{0,1:T(8,128)}, f32[1152,16]{0,1:T(8,128)S(1)}, u32[]{:S(2)}) copy-start(f32[1152,16]{0,1:T(8,128)S(1)} %get-tuple-element.357) | copy-start | bytes 221188
  86.0 86.7 %copy-start.16 = (f32[1152,16]{0,1:T(8,128)}, f32[1152,16]{0,1:T(8,128)S(1)}, u32[]{:S(2)}) copy-start(f32[1152,16]{0,1:T(8,128)S(1)} %get-tuple-element.358) | copy-start | bytes 221188
  312.6 93.0 %all-gather.15.cloned.1.call-start = ((), (), s32[]{:S(2)}) async-start(), calls=%async_computation.11 | async-start | bytes 3538944 | tf_op jit(solution)/shard_map/all_gather | solution.py:156
  313.2 145.8 %all-gather.17.cloned.1.call-start = ((), (), s32[]{:S(2)}) async-start(), calls=%async_computation.12 | async-start | bytes 4456448 | tf_op jit(solution)/shard_map/all_gather | solution.py:139
  314.0 184.7 %all-gather.13.cloned.1.call-start = ((), (), s32[]{:S(2)}) async-start(), calls=%async_computation.10 | async-start | bytes 1114112 | tf_op jit(solution)/shard_map/all_gather | solution.py:138
  370.7 203.5 %reduce-scatter.23.cloned.1.call-start = ((), (), s32[]{:S(2)}) async-start(), calls=%async_computation.21 | async-start | bytes 4456448 | tf_op jit(solution)/shard_map/reduce_scatter | solution.py:310
  498.5 350.1 %all-gather.19.cloned.1.call-start = ((), (), s32[]{:S(2)}) async-start(), calls=%async_computation.13 | async-start | bytes 4456448 | tf_op jit(solution)/shard_map/all_gather | solution.py:140
  576.6 315.0 %reduce-scatter.13.cloned.1.call-start = ((), (), s32[]{:S(2)}) async-start(), calls=%async_computation.16 | async-start | bytes 3538944 | tf_op jit(solution)/shard_map/reduce_scatter | solution.py:269
  848.5 71.5 %reduce-scatter.15.cloned.1.call-start = ((), (), s32[]{:S(2)}) async-start(), calls=%async_computation.17 | async-start | bytes 3538944 | tf_op jit(solution)/shard_map/reduce_scatter | solution.py:272
  869.2 87.6 %reduce-scatter.11.cloned.1.call-start = ((), (), s32[]{:S(2)}) async-start(), calls=%async_computation.14 | async-start | bytes 3538944 | tf_op jit(solution)/shard_map/reduce_scatter | solution.py:226
  880.6 146.7 %reduce-scatter.17.cloned.1.call-start = ((), (), s32[]{:S(2)}) async-start(), calls=%async_computation.18 | async-start | bytes 3342336 | tf_op jit(solution)/shard_map/reduce_scatter | solution.py:301
  888.9 274.1 %reduce-scatter.25.cloned.1.call-start = ((), (), s32[]{:S(2)}) async-start(), calls=%async_computation.22 | async-start | bytes 540672
  964.7 270.8 %reduce-scatter.21.cloned.1.call-start = ((), (), s32[]{:S(2)}) async-start(), calls=%async_computation.20 | async-start | bytes 4456448 | tf_op jit(solution)/shard_map/reduce_scatter | solution.py:307
  974.6 189.2 %copy-start.38 = (f32[13,32]{1,0:T(8,128)S(1)}, f32[13,32]{1,0:T(8,128)}, u32[]{:S(2)}) copy-start(f32[13,32]{1,0:T(8,128)} %param.29) | copy-start | bytes 4996
  974.6 189.2 %copy-start.39 = (f32[13,32]{1,0:T(8,128)S(1)}, f32[13,32]{1,0:T(8,128)}, u32[]{:S(2)}) copy-start(f32[13,32]{1,0:T(8,128)} %param.39) | copy-start | bytes 4996
  974.6 189.2 %copy-start.40 = (f32[13,32]{1,0:T(8,128)S(1)}, f32[13,32]{1,0:T(8,128)}, u32[]{:S(2)}) copy-start(f32[13,32]{1,0:T(8,128)} %param.34) | copy-start | bytes 4996
  974.6 260.8 %copy-start.10 = (f32[64,2048]{1,0:T(8,128)S(1)}, f32[64,2048]{1,0:T(8,128)}, u32[]{:S(2)}) copy-start(f32[64,2048]{1,0:T(8,128)} %param.27) | copy-start | bytes 1572868
  974.6 260.8 %copy-start.21 = (f32[64,2048]{1,0:T(8,128)S(1)}, f32[64,2048]{1,0:T(8,128)}, u32[]{:S(2)}) copy-start(f32[64,2048]{1,0:T(8,128)} %param.37) | copy-start | bytes 1572868
  974.7 260.8 %copy-start.22 = (f32[64,2048]{1,0:T(8,128)S(1)}, f32[64,2048]{1,0:T(8,128)}, u32[]{:S(2)}) copy-start(f32[64,2048]{1,0:T(8,128)} %param.32) | copy-start | bytes 1572868
  (38 other events, 889.0 us)
Sparse Core Ops, SparseCore 0:
  83.8 31.9 all-gather.8
  118.5 45.2 all-gather.10
  165.3 34.8 all-gather.20
  312.7 56.2 reduce-scatter.18
  370.5 35.0 all-gather.14
  408.4 50.5 all-gather.16
  462.0 36.4 all-gather.12
  502.8 71.3 reduce-scatter.22
  576.9 49.7 all-gather.18
  848.7 33.6 reduce-scatter.12
  885.3 34.6 reduce-scatter.14
  922.1 34.7 reduce-scatter.10
  961.1 66.1 reduce-scatter.16
  1030.1 132.8 reduce-scatter.24
  1166.7 68.7 reduce-scatter.20
where the time goes:
time: 1260 us; the launch traced here: 1240 us
  waiting for transfers between devices  605 us (48%)
  matrix products  322 us (26%)
  local copies, waits for them, and re-layouts  177 us (14%)
  blocking collectives  71.4 us (6%)
  other arithmetic  52.5 us (4%)
  between operations  14.9 us (1%)
    unnamed x16, waiting for transfers between devices  135 us
    dynamic_update_slice x48, local copies, waits for them, and re-layouts, per_device(): lax.map(attend, (query_items, key_items, value_items, seq_items, idx_items))  95.1 us
    all_gather x1, blocking collectives, per_device(): lax.all_gather(small_params, ('dp', 'tensor'), axis=1, tiled=True)  71.4 us
    reduce_scatter x1, waiting for transfers between devices, per_device(): lax.psum_scatter(up_grad.astype(jnp.bfloat16), 'dp', scatter_dimension=0,...  71 us
    reduce_scatter x1, waiting for transfers between devices, per_device(): lax.psum_scatter(down_grad.astype(jnp.bfloat16), 'dp', scatter_dimension=...  68.7 us
    dot_general x32, matrix products, masked_scores(): jnp.einsum('qd,kd->qk', query_blk, key_all, preferred_element_type=FLOAT)  64.6 us
    reduce_scatter x1, waiting for transfers between devices, per_device(): lax.psum_scatter(proj_grad.astype(jnp.bfloat16), 'dp', scatter_dimension=...  54.2 us
    all_gather x1, waiting for transfers between devices, per_device(): lax.all_gather(shards[2], 'dp', axis=0, tiled=True)  53.4 us
  transfers between devices with their start and end apart: 15, of which 11 were waited for; matrix products, arithmetic and copies ran while one was open for 42% of the time, Pallas kernels for 0%

commit v1 on v0

v1 whole, which is shorter than its diff:
```python
import functools
import math

import jax
import jax.numpy as jnp
from jax import lax
from jax.experimental import pallas as pl
from jax.experimental.pallas import tpu as pltpu
from jax.sharding import PartitionSpec as P

D = 1024
HD = 64
FF = 4096
ROT = 16
STEP = 10

EPS_NORM = 1e-05
BETA_ONE = 0.9
BETA_TWO = 0.95
EPS_ADAM = 1e-08
DECAY = 0.01
SMALL_RATE = 0.3
BFLOAT = jnp.bfloat16
FLOAT = jnp.float32
ROOT_HALF = 1.0 / math.sqrt(2.0)
INV_ROOT_TAU = 1.0 / math.sqrt(2.0 * math.pi)
PAIR = 2 * HD
QB = 128
MASKED = -1e30


def layout(lengths_row, row_count):
    starts = jnp.cumsum(lengths_row) - lengths_row
    row_index = jnp.arange(row_count, dtype=jnp.int32)
    own_start = jnp.max(
        jnp.where(row_index[:, None] >= starts[None, :], starts[None, :], 0), axis=1
    )
    return own_start, row_index - own_start


def rotary_tables(position):
    half = ROT // 2
    lane = jnp.arange(PAIR, dtype=jnp.int32) % HD
    frequency = 10000.0 ** (-(2.0 * jnp.arange(half, dtype=FLOAT)) / ROT)
    angles = position.astype(FLOAT)[:, None] * frequency[None, :]
    cos = jnp.tile(jnp.cos(angles), (1, PAIR // half))
    sin = jnp.tile(jnp.sin(angles), (1, PAIR // half))
    keep = jnp.where(lane[None] < ROT, cos, 1.0)
    from_left = jnp.where((lane[None] >= half) & (lane[None] < ROT), sin, 0.0)
    from_right = jnp.where(lane[None] < half, -sin, 0.0)
    return keep, from_left, from_right


def attention_kernel(
    pre_ref, grad_ref, keep_ref, left_ref, right_ref, start_ref,
    att_ref, dpre_ref,
    q2_ref, g2_ref, k_ref, kt_ref, v_ref, vt_ref, dk_ref, dv_ref,
):
    rows = pre_ref.shape[0]
    blocks = rows // QB
    half = ROT // 2

    def turn(x, sign, at):
        here = pl.ds(at, x.shape[0])
        return (
            x * keep_ref[here, :]
            + sign * (
                pltpu.roll(x, half, 1) * left_ref[here, :]
                + pltpu.roll(x, PAIR - half, 1) * right_ref[here, :]
            )
        )

    first = lax.broadcasted_iota(jnp.int32, (QB, PAIR), 1) < HD
    top = lax.broadcasted_iota(jnp.int32, (PAIR, QB), 0) < HD
    zero = jnp.zeros((QB, PAIR), FLOAT)
    for i in range(blocks):
        here = pl.ds(i * QB, QB)
        q = turn(pre_ref[here, :PAIR].astype(FLOAT), 1.0, i * QB) * (HD ** -0.5)
        q2_ref[pl.ds(2 * i * QB, QB), :] = jnp.where(first, q, zero).astype(BFLOAT)
        q2_ref[pl.ds((2 * i + 1) * QB, QB), :] = jnp.where(first, zero, q).astype(BFLOAT)
        g = grad_ref[here, :].astype(FLOAT)
        g2_ref[pl.ds(2 * i * QB, QB), :] = jnp.where(first, g, zero).astype(BFLOAT)
        g2_ref[pl.ds((2 * i + 1) * QB, QB), :] = jnp.where(first, zero, g).astype(BFLOAT)
        k = turn(pre_ref[here, PAIR:2 * PAIR].astype(FLOAT), 1.0, i * QB)
        k_ref[here, :] = k.astype(BFLOAT)
        kt_ref[:, here] = k.T.astype(BFLOAT)
        v = pre_ref[here, 2 * PAIR:]
        v_ref[here, :] = v
        vt_ref[:, here] = v.astype(FLOAT).T.astype(BFLOAT)

    for i in range(blocks):
        n = (i + 1) * QB
        here = pl.ds(i * QB, QB)
        q2 = q2_ref[pl.ds(2 * i * QB, 2 * QB), :]
        g2 = g2_ref[pl.ds(2 * i * QB, 2 * QB), :]
        s = lax.dot_general(
            k_ref[:n, :], q2, (((1,), (1,)), ((), ())), preferred_element_type=FLOAT
        )
        start = start_ref[:, here]
        start = jnp.concatenate([start, start], axis=1)
        lane = lax.broadcasted_iota(jnp.int32, (QB, 2 * QB), 1)
        row = lax.broadcasted_iota(jnp.int32, (QB, 2 * QB), 0)
        causal = row <= jnp.where(lane < QB, lane, lane - QB)
        tiles = []
        for j in range(i + 1):
            tile = s[j * QB:(j + 1) * QB]
            allowed = None
            if j == 0 or i * QB >= 1024:
                allowed = row + j * QB >= start
            if j == i:
                allowed = causal if allowed is None else allowed & causal
            tiles.append(tile if allowed is None else jnp.where(allowed, tile, MASKED))
        s = jnp.concatenate(tiles, axis=0) if i else tiles[0]
        e = jnp.exp(s - jnp.max(s, axis=0, keepdims=True))
        p = e * (1.0 / jnp.sum(e, axis=0, keepdims=True))
        dp = lax.dot_general(
            v_ref[:n, :], g2, (((1,), (1,)), ((), ())), preferred_element_type=FLOAT
        )
        delta = jnp.sum(dp * p, axis=0, keepdims=True)
        ds = (p * (dp - delta)).astype(BFLOAT)
        p = p.astype(BFLOAT)
        o = jnp.dot(vt_ref[:, :n], p, preferred_element_type=FLOAT)
        o = jnp.where(top, o[:, :QB], o[:, QB:])
        att_ref[here, :] = o.T.astype(BFLOAT)
        dq = jnp.dot(kt_ref[:, :n], ds, preferred_element_type=FLOAT)
        dq = jnp.where(top, dq[:, :QB], dq[:, QB:]) * (HD ** -0.5)
        dpre_ref[here, :PAIR] = turn(dq.T, -1.0, i * QB).astype(BFLOAT)
        dk = jnp.dot(ds, q2, preferred_element_type=FLOAT)
        dv = jnp.dot(p, g2, preferred_element_type=FLOAT)
        if i:
            before = n - QB
            dk_ref[:before, :] += dk[:before]
            dv_ref[:before, :] += dv[:before]
            dk_ref[here, :] = dk[before:]
            dv_ref[here, :] = dv[before:]
        else:
            dk_ref[here, :] = dk
            dv_ref[here, :] = dv

    for i in range(blocks):
        here = pl.ds(i * QB, QB)
        dpre_ref[here, PAIR:2 * PAIR] = turn(dk_ref[here, :], -1.0, i * QB).astype(BFLOAT)
        dpre_ref[here, 2 * PAIR:] = dv_ref[here, :].astype(BFLOAT)


def attention(qkv_pre, d_attended, keep, left, right, start):
    rows, width = d_attended.shape
    pairs = width // PAIR
    whole = lambda p: (0, 0)
    return pl.pallas_call(
        attention_kernel,
        grid=(pairs,),
        in_specs=[
            pl.BlockSpec((rows, 3 * PAIR), lambda p: (0, p)),
            pl.BlockSpec((rows, PAIR), lambda p: (0, p)),
            pl.BlockSpec((rows, PAIR), whole),
            pl.BlockSpec((rows, PAIR), whole),
            pl.BlockSpec((rows, PAIR), whole),
            pl.BlockSpec((1, rows), whole),
        ],
        out_specs=[
            pl.BlockSpec((rows, PAIR), lambda p: (0, p)),
            pl.BlockSpec((rows, 3 * PAIR), lambda p: (0, p)),
        ],
        out_shape=[
            jax.ShapeDtypeStruct((rows, width), BFLOAT),
            jax.ShapeDtypeStruct((rows, 3 * width), BFLOAT),
        ],
        scratch_shapes=[
            pltpu.VMEM((2 * rows, PAIR), BFLOAT),
            pltpu.VMEM((2 * rows, PAIR), BFLOAT),
            pltpu.VMEM((rows, PAIR), BFLOAT),
            pltpu.VMEM((PAIR, rows), BFLOAT),
            pltpu.VMEM((rows, PAIR), BFLOAT),
            pltpu.VMEM((PAIR, rows), BFLOAT),
            pltpu.VMEM((rows, PAIR), FLOAT),
            pltpu.VMEM((rows, PAIR), FLOAT),
        ],
        compiler_params=pltpu.CompilerParams(vmem_limit_bytes=32 * 1024 * 1024),
        cost_estimate=pl.CostEstimate(
            flops=14 * rows * rows * width // 2 * 4,
            bytes_accessed=rows * width * 16 + rows * PAIR * 12,
            transcendentals=rows * rows * (width // HD) // 2,
        ),
        name="attention",
    )(qkv_pre, d_attended, keep, left, right, start)


def flip_kernel(x_ref, o_ref):
    x = x_ref[...]
    pad = jnp.zeros((o_ref.shape[1] - x.shape[0], x.shape[1]), x.dtype)
    o_ref[...] = jnp.concatenate([x, pad], axis=0).T


def flip(x):
    return pl.pallas_call(
        flip_kernel,
        out_shape=jax.ShapeDtypeStruct((PAIR, PAIR), x.dtype),
        name="flip",
    )(x)[:, :x.shape[0]]


def adamw(weight, moment, second, gradient, step_rate, decay_rate):
    moment = BETA_ONE * moment + (1.0 - BETA_ONE) * gradient
    second = BETA_TWO * second + (1.0 - BETA_TWO) * gradient * gradient
    moment_hat = moment / (1.0 - BETA_ONE**STEP)
    second_hat = second / (1.0 - BETA_TWO**STEP)
    weight = weight - step_rate * (
        moment_hat / (jnp.sqrt(second_hat) + EPS_ADAM) + decay_rate * weight
    )
    return (moment, second, weight)


def mm(a, b):
    return jnp.dot(a, b, preferred_element_type=FLOAT)


def mm_nt(a, b):
    return lax.dot_general(a, b, (((1,), (1,)), ((), ())), preferred_element_type=FLOAT)


def mm_tn(a, b):
    return lax.dot_general(a, b, (((0,), (0,)), ((), ())), preferred_element_type=FLOAT)


def turn_order(index, chips):
    if chips == 8:
        return jnp.where(index < 4, 2 * index, 15 - 2 * index)
    return jnp.where(index < chips // 2, index, 3 * chips // 2 - 1 - index)


class Ring:
    def __init__(self, devices):
        self.n = n = devices // 2
        assert n & (n - 1) == 0
        order = [2 * i if i < 4 else 15 - 2 * i for i in range(n)]
        if n != 8:
            order = [i if i < n // 2 else 3 * n // 2 - 1 - i for i in range(n)]
        me = lax.axis_index("dp")
        self.core = me & 1
        chip = lax.shift_right_logical(me, 1)
        if n == 8:
            z = lax.shift_right_logical(chip, 1)
            self.place = jnp.where(chip & 1 == 0, z, 7 - z)
        else:
            self.place = turn_order(chip, n)
        hop = lambda step: [
            (2 * order[i] + k, 2 * order[(i + step) % n] + k) for i in range(n) for k in range(2)
        ]
        self.up_pairs, self.down_pairs = hop(1), hop(n - 1)
        self.twin_pairs = [(2 * c + k, 2 * c + 1 - k) for c in range(n) for k in range(2)]

    def up(self, x):
        return lax.ppermute(x, "dp", self.up_pairs)

    def down(self, x):
        return lax.ppermute(x, "dp", self.down_pairs)

    def twin(self, x):
        return lax.ppermute(x, "dp", self.twin_pairs)

    def chip_at(self, offset):
        return turn_order((self.place + (offset + self.n)) & (self.n - 1), self.n)

    def reduce_scatter(self, grad):
        n, columns = self.n, grad.shape[1]
        rows = grad.shape[0] // (2 * n)
        cut = rows // 2
        parts = grad.reshape(n, 2, rows, columns)
        theirs = lax.dynamic_index_in_dim(parts, 1 - self.core, 1, keepdims=False)
        came = self.twin(theirs)

        def here(offset):
            chip = self.chip_at(offset)
            own = lax.dynamic_slice(parts, (chip, self.core, 0, 0), (1, 1, rows, columns))
            twin = lax.dynamic_slice(came, (chip, 0, 0), (1, rows, columns))
            return own.reshape(rows, columns).astype(FLOAT) + twin[0].astype(FLOAT)

        far = n // 2
        split = here(far)
        going_up = self.up(split[:cut].astype(BFLOAT)).astype(FLOAT)
        going_down = self.down(split[cut:].astype(BFLOAT)).astype(FLOAT)
        for step in range(far - 1, 0, -1):
            up_sum, down_sum = here(step), here(-step)
            if step == far - 1:
                going_up = jnp.concatenate([up_sum[:cut] + going_up, up_sum[cut:]], axis=0)
                going_down = jnp.concatenate([down_sum[:cut], down_sum[cut:] + going_down], axis=0)
            else:
                going_up, going_down = up_sum + going_up, down_sum + going_down
            going_up = self.up(going_up.astype(BFLOAT)).astype(FLOAT)
            going_down = self.down(going_down.astype(BFLOAT)).astype(FLOAT)
        return here(0) + going_up + going_down

    def all_gather(self, shard):
        n = self.n
        rows, columns = shard.shape
        cut = rows // 2
        full = jnp.zeros((n, 2, rows, columns), shard.dtype)

        def put(full, offset, block, core, row):
            return lax.dynamic_update_slice(
                full, block[None, None], (self.chip_at(offset), core, row, 0)
            )

        def put_both(full, offset, block, row=0):
            full = put(full, offset, block, self.core, row)
            return put(full, offset, self.twin(block), 1 - self.core, row)

        full = put_both(full, 0, shard)
        from_below, from_above = shard, shard
        for step in range(1, n // 2):
            from_below, from_above = self.up(from_below), self.down(from_above)
            full = put_both(full, -step, from_below)
            full = put_both(full, step, from_above)
        full = put_both(full, n // 2, self.up(from_below[:cut]))
        full = put_both(full, n // 2, self.down(from_above[cut:]), cut)
        return full.reshape(2 * n * rows, columns)


def swap(x):
    return lax.ppermute(x, "tensor", [(0, 1), (1, 0)])


def gather_rows(part, ways, axis=0):
    if ways != 2:
        return lax.all_gather(part, "tensor", axis=axis, tiled=True)
    came = swap(part)
    first = lax.axis_index("tensor") == 0
    return jnp.concatenate(
        [jnp.where(first, part, came), jnp.where(first, came, part)], axis=axis
    )


def scatter_rows(pieces, ways):
    if ways == 2:
        return swap(pieces[0].astype(BFLOAT)).astype(FLOAT) + pieces[1]
    return lax.psum_scatter(
        pieces[0].astype(BFLOAT), "tensor", scatter_dimension=0, tiled=True
    ).astype(FLOAT)


def per_device(
    ways, groups,
    tokens, cotangent, lengths,
    qkv_weight, proj_weight, up_weight, down_weight, small_params,
    qkv_first, proj_first, up_first, down_first, small_first,
    qkv_second, proj_second, up_second, down_second, small_second,
):
    ring = Ring(groups)
    tensor_rank = lax.axis_index("tensor")
    in_rows = qkv_weight.shape[0]
    local_width = qkv_weight.shape[2]
    hidden_width = up_weight.shape[1]
    pairs = local_width // PAIR
    own_rows = tokens.shape[0]
    row_count = own_rows * ways
    small_rows = small_params.shape[0]
    qkv_width = 3 * local_width
    att_width = qkv_width + local_width

    def pair_major(t):
        return (
            t.reshape(t.shape[0], 3, pairs, PAIR)
            .transpose(0, 2, 1, 3)
            .reshape(t.shape[0], qkv_width)
        )

    def from_pair_major(t):
        return (
            t.reshape(t.shape[0], pairs, 3, PAIR)
            .transpose(0, 2, 1, 3)
            .reshape(t.shape[0], 3, local_width)
        )

    small_here = gather_rows(small_params, ways, axis=1).T
    small_high = lax.reduce_precision(small_here, 8, 7)
    small_shard = jnp.concatenate(
        [
            small_high.astype(BFLOAT),
            (small_here - small_high).astype(BFLOAT),
            jnp.zeros((in_rows, PAIR - 2 * small_rows), BFLOAT),
        ],
        axis=1,
    )
    att_shard = jnp.concatenate(
        [pair_major(qkv_weight.astype(BFLOAT)), proj_weight.T.astype(BFLOAT), small_shard], axis=1
    )
    mlp_shard = jnp.concatenate(
        [up_weight.astype(BFLOAT), down_weight.T.astype(BFLOAT)], axis=1
    )
    rows_in = gather_rows(tokens, ways)
    later_cotangent, rows_in = lax.optimization_barrier((cotangent, rows_in))
    dy = gather_rows(later_cotangent, ways)
    att_full = ring.all_gather(att_shard)
    mlp_full = lax.all_gather(mlp_shard, "dp", axis=0, tiled=True)
    qkv_full, proj_t = att_full[:, :qkv_width], att_full[:, qkv_width:att_width]
    small = att_full[:, att_width:att_width + 2 * small_rows].astype(FLOAT).T
    small = small[:small_rows] + small[small_rows:]

    bias_qkv = pair_major(
        lax.dynamic_slice_in_dim(small[4:7], tensor_rank * local_width, local_width, 1)[None]
    )[0]
    bias_up = lax.dynamic_slice_in_dim(
        small[8:12].reshape(4 * D), tensor_rank * hidden_width, hidden_width, 0
    )

    inputs = rows_in.astype(FLOAT)
    average = jnp.mean(inputs, axis=-1, keepdims=True)
    centred = inputs - average
    variance = jnp.mean(centred * centred, axis=-1, keepdims=True)
    inv_dev = lax.rsqrt(variance + EPS_NORM)
    xhat = centred * inv_dev
    normed_a = (xhat * small[0] + small[1]).astype(BFLOAT)
    normed_m = (xhat * small[2] + small[3]).astype(BFLOAT)

    start, position = layout(lengths[0], row_count)
    keep, left, right = rotary_tables(position)

    own_at = tensor_rank * own_rows
    cuts = [(own_rows - own_at, own_rows), (own_at, own_rows)] if ways == 2 else [(0, row_count)]
    rows_of = lambda t, cut: lax.dynamic_slice_in_dim(t, cut[0], cut[1], 0)

    qkv_pre = (mm(normed_a, qkv_full) + bias_qkv).astype(BFLOAT)
    d_attended = mm(dy, proj_t).astype(BFLOAT)
    attended, d_qkv = attention(qkv_pre, d_attended, keep, left, right, start[None])
    proj_grad = mm_tn(dy, attended)
    qkv_grad = mm_tn(normed_a, d_qkv)
    qkv_bias_grad = jnp.sum(d_qkv, axis=0, dtype=FLOAT)
    att_grad = jnp.concatenate([qkv_grad.astype(BFLOAT), proj_grad.astype(BFLOAT)], axis=1)
    att_grad, mlp_full = lax.optimization_barrier((att_grad, mlp_full))
    att_own = lax.psum_scatter(att_grad, "dp", scatter_dimension=0, tiled=True).astype(FLOAT)

    up_full, down_t = mlp_full[:, :hidden_width], mlp_full[:, hidden_width:]
    hidden_pre = mm(normed_m, up_full) + bias_up
    cdf = 0.5 * (1.0 + lax.erf(hidden_pre * ROOT_HALF))
    density = jnp.exp(-0.5 * hidden_pre * hidden_pre) * INV_ROOT_TAU
    hidden = (hidden_pre * cdf).astype(BFLOAT)
    d_pre = (mm(dy, down_t) * (cdf + hidden_pre * density)).astype(BFLOAT)
    up_bias_grad = jnp.sum(d_pre, axis=0, dtype=FLOAT)

    summed = scatter_rows(
        [mm_nt(rows_of(attended, c), proj_t) + mm_nt(rows_of(hidden, c), down_t) for c in cuts],
        ways,
    )
    own_inputs = tokens.astype(FLOAT)
    block_out = (own_inputs + summed + small[7] + small[12]).astype(BFLOAT)

    d_a = [mm_nt(rows_of(d_qkv, c), qkv_full) for c in cuts]
    d_m = [mm_nt(rows_of(d_pre, c), up_full) for c in cuts]
    e_own = scatter_rows([a * small[0] + m * small[2] for a, m in zip(d_a, d_m)], ways)
    own_hat = rows_of(xhat, (own_at, own_rows))
    own_inv = rows_of(inv_dev, (own_at, own_rows))
    token_grad = cotangent.astype(FLOAT) + own_inv * (
        e_own
        - jnp.mean(e_own, axis=-1, keepdims=True)
        - own_hat * jnp.mean(e_own * own_hat, axis=-1, keepdims=True)
    )

    out_bias_grad = jnp.sum(cotangent, axis=0, dtype=FLOAT)
    qkv_rows = lax.dynamic_update_slice_in_dim(
        jnp.zeros((3, D), FLOAT),
        from_pair_major(qkv_bias_grad[None])[0],
        tensor_rank * local_width,
        1,
    )
    up_rows = lax.dynamic_update_slice_in_dim(
        jnp.zeros((4 * D,), FLOAT), up_bias_grad, tensor_rank * hidden_width, 0
    )
    with_hat = lambda ds: sum(
        jnp.sum(d * rows_of(xhat, c), axis=0)[None] for d, c in zip(ds, cuts)
    )
    plain = lambda ds: sum(jnp.sum(d, axis=0)[None] for d in ds)
    small_local = jnp.concatenate(
        [
            with_hat(d_a),
            plain(d_a),
            with_hat(d_m),
            plain(d_m),
            qkv_rows,
            out_bias_grad[None],
            up_rows.reshape(4, D),
            out_bias_grad[None],
        ],
        axis=0,
    )
    small_both = small_local + swap(small_local) if ways == 2 else lax.psum(small_local, "tensor")
    small_columns = jnp.pad(small_both.T, ((0, 0), (0, PAIR - small_rows))).astype(BFLOAT)

    down_own = ring.reduce_scatter(mm_tn(dy, hidden).astype(BFLOAT))
    up_own = ring.reduce_scatter(
        jnp.concatenate([mm_tn(normed_m, d_pre).astype(BFLOAT), small_columns], axis=1)
    )
    small_width = small_params.shape[1]
    small_grad = lax.dynamic_slice_in_dim(
        flip(up_own[:, hidden_width:])[:small_rows],
        tensor_rank * small_width,
        small_width,
        1,
    )
    qkv_owned = from_pair_major(att_own[:, :qkv_width])
    proj_owned = att_own[:, qkv_width:].T
    up_owned = up_own[:, :hidden_width]
    down_owned = down_own.T
    qkv_new = adamw(qkv_weight, qkv_first, qkv_second, qkv_owned, D ** (-0.5), DECAY)
    proj_new = adamw(proj_weight, proj_first, proj_second, proj_owned, (D // 64) ** (-0.5), DECAY)
    up_new = adamw(up_weight, up_first, up_second, up_owned, D ** (-0.5), DECAY)
    down_new = adamw(down_weight, down_first, down_second, down_owned, FF ** (-0.5), DECAY)
    small_new = adamw(small_params, small_first, small_second, small_grad, SMALL_RATE, 0.0)
    return (block_out, token_grad) + qkv_new + proj_new + up_new + down_new + small_new


def solution(mesh):
    rows = P(("dp", "tensor"), None)
    weights = (P("dp", None, "tensor"), P("tensor", "dp"), P("dp", "tensor"), P("tensor", "dp"))
    small = P(None, ("dp", "tensor"))
    return jax.shard_map(
        functools.partial(per_device, mesh.shape["tensor"], mesh.shape["dp"]),
        mesh=mesh,
        in_specs=(rows, rows, P("dp", None)) + 3 * (weights + (small,)),
        out_specs=(rows, rows) + tuple(w for w in weights + (small,) for _ in range(3)),
        check_vma=False,
    )
```

time: 1260 us -> 397 us (0.32)
  waiting for transfers between devices: 605 us -> 136 us
  matrix products: 322 us -> 86.9 us
  local copies, waits for them, and re-layouts: 177 us -> 28.5 us
  blocking collectives: 71.4 us -> 0 us
  starting transfers between devices: 0.79 us -> 50.3 us
  Pallas kernels: 0 us -> 34.8 us
  other arithmetic: 52.5 us -> 37.2 us
    reduce_scatter x7 -> x1, waiting for transfers between devices: 305 us -> 0.01 us  [per_device(): lax.psum_scatter(att_grad, 'dp', scatter_dimension=0, tiled=True)]
    dot_general x124 -> x16, matrix products: 322 us -> 86.9 us  [the longest x8 35.3 us: mm_nt(): lax.dot_general(a, b, (((1,), (1,)), ((), ())), preferred_element_type=FL...]
    all_gather x7 -> x1, waiting for transfers between devices: 165 us -> 0.01 us  [per_device(): mlp_full = lax.all_gather(mlp_shard, 'dp', axis=0, tiled=True)]
    ppermute x0 -> x41, waiting for transfers between devices: none -> 136 us  [the longest x12 58.9 us: up(): return lax.ppermute(x, 'dp', self.up_pairs)]
    unnamed x16 -> x2, waiting for transfers between devices: 135 us -> 0.03 us
    dynamic_update_slice x50 -> x20, local copies, waits for them, and re-layouts: 95.5 us -> 2.72 us  [the longest x1 1.45 us: per_device(): lax.dynamic_update_slice_in_dim(jnp.zeros((4 * D,), FLOAT), up_bias_grad,...]
    all_gather x1 -> x0, blocking collectives: 71.4 us -> none  [per_device(): lax.all_gather(small_params, ('dp', 'tensor'), axis=1, tiled=True)]
    ppermute x0 -> x41, starting transfers between devices: none -> 50.2 us  [the longest x12 31.4 us: up(): return lax.ppermute(x, 'dp', self.up_pairs)]
  transfers between devices with their start and end apart: 15 -> 43, of which waited for: 11 -> 22; matrix products, arithmetic and copies ran while one was open for 42% -> 27% of each run, Pallas kernels for 0% -> 9%
where the time goes in v1:
time: 397 us; the launch traced here: 390 us
  waiting for transfers between devices  136 us (34%)
  matrix products  86.9 us (22%)
  starting transfers between devices  50.3 us (13%)
  other arithmetic  37.2 us (9%)
  Pallas kernels  34.8 us (9%)
  local copies, waits for them, and re-layouts  28.5 us (7%)
  between operations  15.7 us (4%)
    ppermute x12, waiting for transfers between devices, up(): return lax.ppermute(x, 'dp', self.up_pairs)  58.9 us
    ppermute x6, waiting for transfers between devices, swap(): return lax.ppermute(x, 'tensor', [(0, 1), (1, 0)])  38.2 us
    ppermute x12, waiting for transfers between devices, down(): return lax.ppermute(x, 'dp', self.down_pairs)  38.1 us
    dot_general x8, matrix products, mm_nt(): lax.dot_general(a, b, (((1,), (1,)), ((), ())), preferred_element_type=FL...  35.3 us
    pallas_call x1, Pallas kernels, attention(): pl.pallas_call(attention_kernel, grid=(pairs,), in_specs=[pl.BlockSpec((r...  33.3 us
    ppermute x12, starting transfers between devices, up(): return lax.ppermute(x, 'dp', self.up_pairs)  31.4 us
    dot_general x4, matrix products, mm_tn(): lax.dot_general(a, b, (((0,), (0,)), ((), ())), preferred_element_type=FL...  27.2 us
    dot_general x4, matrix products, mm(): return jnp.dot(a, b, preferred_element_type=FLOAT)  24.4 us
  transfers between devices with their start and end apart: 43, of which 22 were waited for; matrix products, arithmetic and copies ran while one was open for 27% of the time, Pallas kernels for 9%

profile of v1, /device:TPU:0, one launch (start us, length us, event | category | flops | bytes accessed | tf_op | source)
XLA Modules:
  0.0 389.7 jit_solution(18397716968733855231)
XLA Ops:
  22.6 10.8 %collective-permute-done.3 = bf16[64,2176]{1,0:T(8,128)(2,1)S(1)} collective-permute-done((bf16[64,2176]{1,0:T(8,128)(2,1)S(1)}, bf16[64,2176]{1,0:T(8,128)(2,1)S(1)}, u32[]{:S(2)}, u32[]{:S(2)}) %collective-permute-start.3) | collective-permute-done | bytes 278560 | tf_op jit(solution)/shard_map/ppermute | solution.py:254
  33.4 5.2 %collective-permute-start.7 = (bf16[64,2176]{1,0:T(8,128)(2,1)S(1)}, bf16[64,2176]{1,0:T(8,128)(2,1)S(1)}, u32[]{:S(2)}, u32[]{:S(2)}) collective-permute-start(bf16[64,2176]{1,0:T(8,128)(2,1)S(1)} %collective-permute-done.3), channel_id=1, source_target_pairs={{0,8},{2,10},{8,16},{10,18},{16,24},{18,26},{24,28},{26,30},{28,20... | collective-permute-start | bytes 835592 | tf_op jit(solution)/shard_map/ppermute | solution.py:254
  41.4 9.9 %collective-permute-done.7 = bf16[64,2176]{1,0:T(8,128)(2,1)S(1)} collective-permute-done((bf16[64,2176]{1,0:T(8,128)(2,1)S(1)}, bf16[64,2176]{1,0:T(8,128)(2,1)S(1)}, u32[]{:S(2)}, u32[]{:S(2)}) %collective-permute-start.7) | collective-permute-done | bytes 278560 | tf_op jit(solution)/shard_map/ppermute | solution.py:254
  54.5 8.4 %collective-permute-done.11 = bf16[64,2176]{1,0:T(8,128)(2,1)S(1)} collective-permute-done((bf16[64,2176]{1,0:T(8,128)(2,1)S(1)}, bf16[64,2176]{1,0:T(8,128)(2,1)S(1)}, u32[]{:S(2)}, u32[]{:S(2)}) %collective-permute-start.11) | collective-permute-done | bytes 278560 | tf_op jit(solution)/shard_map/ppermute | solution.py:254
  73.3 7.5 %collective-permute-done.17 = bf16[32,2176]{1,0:T(8,128)(2,1)S(1)} collective-permute-done((bf16[32,2176]{1,0:T(8,128)(2,1)S(1)}, bf16[32,2176]{1,0:T(8,128)(2,1)S(1)}, u32[]{:S(2)}, u32[]{:S(2)}) %collective-permute-start.17) | collective-permute-done | bytes 139296 | tf_op jit(solution)/shard_map/ppermute | solution.py:257
  97.0 4.7 %fusion.5.pre_ref = bf16[1152,1536]{1,0:T(8,128)(2,1)S(1)} fusion(f32[1536]{0:T(1024)S(1)} %add.578, bf16[1024,2176]{1,0:T(8,128)(2,1)S(1)} %bitcast.229, f32[1024]{0:T(1024)S(1)} %get-tuple-element.43, f32[1024]{0:T(1024)S(1)} %get-tuple-element.44, bf16[1152,1024]{1,0:T(8,128)(2,1)S(1)} %pad_maximum_fusion.1, f32[1152]{0:T(1024)S(1)} %add_rsqrt_fusion, ...), kind=kOutput, calls=%fused_computation.13 | convolution fusion | flops 3634495488 | bytes 9076736 | tf_op jit(solution)/shard_map/dot_general | solution.py:215
  101.8 17.2 %collective-permute-done.19 = bf16[576,1024]{1,0:T(8,128)(2,1)S(1)} collective-permute-done((bf16[576,1024]{1,0:T(8,128)(2,1)S(1)}, bf16[576,1024]{1,0:T(8,128)(2,1)S(1)}, u32[]{:S(2)}, u32[]{:S(2)}) %collective-permute-start.19) | collective-permute-done | bytes 1179680 | tf_op jit(solution)/shard_map/ppermute | solution.py:321
  121.4 33.3 %attention.1 = (bf16[1152,512]{1,0:T(8,128)(2,1)S(1)}, bf16[1152,1536]{1,0:T(8,128)(2,1)S(1)}) custom-call(bf16[1152,1536]{1,0:T(8,128)(2,1)S(1)} %fusion.5.pre_ref, bf16[1152,512]{1,0:T(8,128)(2,1)S(1)} %convolution_convert_fusion.3.grad_ref, f32[1152,128]{1,0:T(8,128)S(1)} %copy-done.2, f32[1152,128]{1,0:T(8,128)S(1)} %copy-done.1, ...), custom_call_target="tpu_custom_call" | custom-call | flops 19025362944 | bytes 11206656 | tf_op jit(solution)/shard_map/attention/pallas_call | solution.py:150
  162.0 5.2 %convolution_convert_fusion.2 = bf16[1024,1536]{1,0:T(8,128)(2,1)S(1)} fusion(bf16[1152,1536]{1,0:T(8,128)(2,1)S(1)} %get-tuple-element.26, f32[1024]{0:T(1024)S(1)} %copy-done.53, f32[1024]{0:T(1024)S(1)} %copy-done.48, bf16[1152,1024]{1,0:T(8,128)(2,1)S(1)} %copy-done.6, f32[1152]{0:T(1024)S(1)} %copy-done.37, f32[1152]{0:T(1024)S(1)} %broadcast_multiply_fusion), kind=kOutput, calls=%fused_computation.27 | convolution fusion | flops 3632529408 | bytes 9061376 | tf_op jit(solution)/shard_map/dot_general | solution.py:223
  169.9 5.3 %fusion.23 = f32[576,1024]{1,0:T(8,128)} fusion(bf16[1024,2176]{1,0:T(8,128)(2,1)} %bitcast.224, bf16[1152,1536]{1,0:T(8,128)(2,1)S(1)} %get-tuple-element.26, s32[]{:T(128)S(6)} %select_n.290), kind=kOutput, calls=%fused_computation.43 | convolution fusion | flops 1811939328 | bytes 7274500 | tf_op jit(solution)/shard_map/dot_general | solution.py:219
  175.2 9.1 %multiply_convert_fusion = (bf16[1152,2048]{1,0:T(8,128)(2,1)S(1)}, f32[1152,2048]{1,0:T(8,128)S(1)}) fusion(f32[2048]{0:T(1024)} %dynamic_slice.149, bf16[1024,4096]{1,0:T(8,128)(2,1)} %all-gather.2.cloned.1.call-done, f32[1024]{0:T(1024)} %get-tuple-element.41, f32[1024]{0:T(1024)} %get-tuple-element.42, f32[1152]{0:T(1024)S(1)} %copy-done.37, ...), kind=kOutput, calls=%fused_computation.7 | convolution fusion | flops 4853071872 | bytes 20734976 | tf_op jit(solution)/shard_map/dot_general | solution.py:215
  188.4 7.3 %convolution_convert_fusion = bf16[1024,2048]{1,0:T(8,128)(2,1)} fusion(bf16[1152,2048]{1,0:T(8,128)(2,1)S(1)} %get-tuple-element.87, bf16[576,1024]{1,0:T(8,128)(2,1)S(1)} %copy-done.22, bf16[576,1024]{1,0:T(8,128)(2,1)S(1)} %copy-done.20), kind=kOutput, calls=%fused_computation.25 | convolution fusion | flops 4838653952 | bytes 11272192 | tf_op jit(solution)/shard_map/dot_general | solution.py:223
  195.7 9.2 %convert_reduce_fusion = (f32[2048]{0:T(1024)S(1)}, bf16[1152,2048]{1,0:T(8,128)(2,1)S(1)}) fusion(f32[1152,2048]{1,0:T(8,128)S(1)} %get-tuple-element.88, bf16[1024,4096]{1,0:T(8,128)(2,1)S(1)} %copy-done.54, bf16[576,1024]{1,0:T(8,128)(2,1)S(1)} %copy-done.22, bf16[576,1024]{1,0:T(8,128)(2,1)S(1)} %copy-done.20), kind=kOutput, calls=%fused_computation.6 | convolution fusion | flops 4864866304 | bytes 20717568 | tf_op jit(solution)/shard_map/dot_general | solution.py:215
  221.9 11.0 %convolution_convert_fusion.1 = bf16[1024,2048]{1,0:T(8,128)(2,1)} fusion(bf16[1152,2048]{1,0:T(8,128)(2,1)} %copy-done.59, f32[1024]{0:T(1024)S(1)} %copy-done.51, f32[1024]{0:T(1024)S(1)} %copy-done.46, bf16[1152,1024]{1,0:T(8,128)(2,1)S(1)} %copy-done.7, f32[1152]{0:T(1024)S(1)} %copy-done.37, f32[1152]{0:T(1024)S(1)} %broadcast_multiply_fusion), kind=kOutput, calls=%fused_computation.26 | convolution fusion | flops 4841013248 | bytes 11289600 | tf_op jit(solution)/shard_map/dot_general | solution.py:223
  232.9 8.0 %collective-permute-done.21 = bf16[576,1024]{1,0:T(8,128)(2,1)} collective-permute-done((bf16[576,1024]{1,0:T(8,128)(2,1)}, bf16[576,1024]{1,0:T(8,128)(2,1)}, u32[]{:S(2)}, u32[]{:S(2)}) %collective-permute-start.21) | collective-permute-done | bytes 1179680 | tf_op jit(solution)/shard_map/ppermute | solution.py:321
  241.0 5.5 %multiply_reduce_fusion = (f32[1024]{0:T(1024)S(1)}, f32[1024]{0:T(1024)S(1)}, f32[1024]{0:T(1024)S(1)}, f32[576]{0:T(1024)S(1)}, f32[1024]{0:T(1024)S(1)}, /*in...) fusion(f32[576,1024]{1,0:T(8,128)S(1)} %copy-done.57, ...), kind=kOutput, calls=%fused_computation.48 | convolution fusion | flops 1823726592 | bytes 20297728 | tf_op jit(solution)/shard_map/dot_general | solution.py:219
  263.7 5.5 %fusion.12 = f32[576,1024]{1,0:T(8,128)S(1)} fusion(bf16[1024,4096]{1,0:T(8,128)(2,1)} %all-gather.2.cloned.1.call-done, bf16[1152,2048]{1,0:T(8,128)(2,1)} %copy-done.60, s32[]{:T(128)S(6)} %select_n.292), kind=kOutput, calls=%fused_computation.29 | convolution fusion | flops 2415919104 | bytes 8912900 | tf_op jit(solution)/shard_map/dot_general | solution.py:219
  272.2 13.0 %collective-permute-done.20 = bf16[576,1024]{1,0:T(8,128)(2,1)S(1)} collective-permute-done((bf16[576,1024]{1,0:T(8,128)(2,1)}, bf16[576,1024]{1,0:T(8,128)(2,1)S(1)}, u32[]{:S(2)}, u32[]{:S(2)}) %collective-permute-start.20) | collective-permute-done | bytes 1179680 | tf_op jit(solution)/shard_map/ppermute | solution.py:321
  292.7 10.7 %collective-permute-done.34 = bf16[64,2048]{1,0:T(8,128)(2,1)S(1)} collective-permute-done((bf16[64,2048]{1,0:T(8,128)(2,1)S(1)}, bf16[64,2048]{1,0:T(8,128)(2,1)S(1)}, u32[]{:S(2)}, u32[]{:S(2)}) %collective-permute-start.34) | collective-permute-done | bytes 262176 | tf_op jit(solution)/shard_map/ppermute | solution.py:254
  311.9 5.1 %collective-permute-done.35 = bf16[64,2048]{1,0:T(8,128)(2,1)S(1)} collective-permute-done((bf16[64,2048]{1,0:T(8,128)(2,1)S(1)}, bf16[64,2048]{1,0:T(8,128)(2,1)S(1)}, u32[]{:S(2)}, u32[]{:S(2)}) %collective-permute-start.35) | collective-permute-done | bytes 262176 | tf_op jit(solution)/shard_map/ppermute | solution.py:254
  318.3 5.4 %collective-permute-done.25 = bf16[64,2176]{1,0:T(8,128)(2,1)S(1)} collective-permute-done((bf16[64,2176]{1,0:T(8,128)(2,1)S(1)}, bf16[64,2176]{1,0:T(8,128)(2,1)S(1)}, u32[]{:S(2)}, u32[]{:S(2)}) %collective-permute-start.25) | collective-permute-done | bytes 278560 | tf_op jit(solution)/shard_map/ppermute | solution.py:254
  333.9 8.0 %collective-permute-done.28 = bf16[32,2176]{1,0:T(8,128)(2,1)S(1)} collective-permute-done((bf16[32,2176]{1,0:T(8,128)(2,1)S(1)}, bf16[32,2176]{1,0:T(8,128)(2,1)S(1)}, u32[]{:S(2)}, u32[]{:S(2)}) %collective-permute-start.28) | collective-permute-done | bytes 139296 | tf_op jit(solution)/shard_map/ppermute | solution.py:257
  347.9 7.4 %collective-permute-done.29 = bf16[64,2176]{1,0:T(8,128)(2,1)S(1)} collective-permute-done((bf16[64,2176]{1,0:T(8,128)(2,1)S(1)}, bf16[64,2176]{1,0:T(8,128)(2,1)S(1)}, u32[]{:S(2)}, u32[]{:S(2)}) %collective-permute-start.29) | collective-permute-done | bytes 278560 | tf_op jit(solution)/shard_map/ppermute | solution.py:257
  356.1 4.8 %collective-permute-done.39 = bf16[64,2048]{1,0:T(8,128)(2,1)S(1)} collective-permute-done((bf16[64,2048]{1,0:T(8,128)(2,1)S(1)}, bf16[64,2048]{1,0:T(8,128)(2,1)S(1)}, u32[]{:S(2)}, u32[]{:S(2)}) %collective-permute-start.39) | collective-permute-done | bytes 262176 | tf_op jit(solution)/shard_map/ppermute | solution.py:257
  (347 shorter events, 156.5 us)
Async XLA Ops:
  7.2 168.0 %all-gather.2.cloned.1.call-start = ((), (), s32[]{:S(2)}) async-start(), calls=%async_computation.1 | async-start | bytes 8912896 | tf_op jit(solution)/shard_map/all_gather | solution.py:395
  10.2 79.4 %collective-permute-start = (bf16[576,1024]{1,0:T(8,128)(2,1)}, bf16[576,1024]{1,0:T(8,128)(2,1)S(1)}, u32[]{:S(2)}, u32[]{:S(2)}) collective-permute-start(bf16[576,1024]{1,0:T(8,128)(2,1)} %param.18), channel_id=1, source_target_pairs={{0,1},{1,0},{2,3},{3,2},{4,5},{5,4},{6,7},{7,6},{8,9},{9,8},{10,11... | collective-permute-start | bytes 3538952 | tf_op jit(solution)/shard_map/ppermute | solution.py:321
  13.3 365.5 %reduce-scatter.2.cloned.1.call-start = ((), (), s32[]{:S(2)}) async-start(), calls=%async_computation.2 | async-start | bytes 4456448 | tf_op jit(solution)/shard_map/reduce_scatter | solution.py:431
  19.8 21.5 %collective-permute-start.2 = (bf16[64,2176]{1,0:T(8,128)(2,1)S(1)}, bf16[64,2176]{1,0:T(8,128)(2,1)S(1)}, u32[]{:S(2)}, u32[]{:S(2)}) collective-permute-start(bf16[64,2176]{1,0:T(8,128)(2,1)S(1)} %concatenate.42), channel_id=1, source_target_pairs={{0,2},{2,0},{4,6},{6,4},{8,10},{10,8},{12,14},{14,12},{16,18},{18,... | collective-permute-start | bytes 835592 | tf_op jit(solution)/shard_map/ppermute | solution.py:260
  19.9 13.5 %collective-permute-start.3 = (bf16[64,2176]{1,0:T(8,128)(2,1)S(1)}, bf16[64,2176]{1,0:T(8,128)(2,1)S(1)}, u32[]{:S(2)}, u32[]{:S(2)}) collective-permute-start(bf16[64,2176]{1,0:T(8,128)(2,1)S(1)} %concatenate.42), channel_id=1, source_target_pairs={{0,8},{2,10},{8,16},{10,18},{16,24},{18,26},{24,28},{26,30},{28,20... | collective-permute-start | bytes 835592 | tf_op jit(solution)/shard_map/ppermute | solution.py:254
  22.0 19.4 %collective-permute-start.5 = (bf16[64,2176]{1,0:T(8,128)(2,1)S(1)}, bf16[64,2176]{1,0:T(8,128)(2,1)S(1)}, u32[]{:S(2)}, u32[]{:S(2)}) collective-permute-start(bf16[64,2176]{1,0:T(8,128)(2,1)S(1)} %concatenate.42), channel_id=1, source_target_pairs={{0,4},{2,6},{8,0},{10,2},{16,8},{18,10},{24,16},{26,18},{28,24},{3... | collective-permute-start | bytes 835592 | tf_op jit(solution)/shard_map/ppermute | solution.py:257
  33.4 18.0 %collective-permute-start.4 = (bf16[64,2176]{1,0:T(8,128)(2,1)S(1)}, bf16[64,2176]{1,0:T(8,128)(2,1)S(1)}, u32[]{:S(2)}, u32[]{:S(2)}) collective-permute-start(bf16[64,2176]{1,0:T(8,128)(2,1)S(1)} %collective-permute-done.3), channel_id=1, source_target_pairs={{0,2},{2,0},{4,6},{6,4},{8,10},{10,8},{12,14},{14,12},{16,18},{18,... | collective-permute-start | bytes 835592 | tf_op jit(solution)/shard_map/ppermute | solution.py:260
  33.4 17.9 %collective-permute-start.7 = (bf16[64,2176]{1,0:T(8,128)(2,1)S(1)}, bf16[64,2176]{1,0:T(8,128)(2,1)S(1)}, u32[]{:S(2)}, u32[]{:S(2)}) collective-permute-start(bf16[64,2176]{1,0:T(8,128)(2,1)S(1)} %collective-permute-done.3), channel_id=1, source_target_pairs={{0,8},{2,10},{8,16},{10,18},{16,24},{18,26},{24,28},{26,30},{28,20... | collective-permute-start | bytes 835592 | tf_op jit(solution)/shard_map/ppermute | solution.py:254
  51.3 17.7 %collective-permute-start.8 = (bf16[64,2176]{1,0:T(8,128)(2,1)S(1)}, bf16[64,2176]{1,0:T(8,128)(2,1)S(1)}, u32[]{:S(2)}, u32[]{:S(2)}) collective-permute-start(bf16[64,2176]{1,0:T(8,128)(2,1)S(1)} %collective-permute-done.7), channel_id=1, source_target_pairs={{0,2},{2,0},{4,6},{6,4},{8,10},{10,8},{12,14},{14,12},{16,18},{18,... | collective-permute-start | bytes 835592 | tf_op jit(solution)/shard_map/ppermute | solution.py:260
  53.8 15.4 %collective-permute-start.10 = (bf16[64,2176]{1,0:T(8,128)(2,1)S(1)}, bf16[64,2176]{1,0:T(8,128)(2,1)S(1)}, u32[]{:S(2)}, u32[]{:S(2)}) collective-permute-start(bf16[64,2176]{1,0:T(8,128)(2,1)S(1)} %collective-permute-done.9), channel_id=1, source_target_pairs={{0,2},{2,0},{4,6},{6,4},{8,10},{10,8},{12,14},{14,12},{16,18},{18,... | collective-permute-start | bytes 835592 | tf_op jit(solution)/shard_map/ppermute | solution.py:260
  54.1 14.8 %collective-permute-start.13 = (bf16[64,2176]{1,0:T(8,128)(2,1)S(1)}, bf16[64,2176]{1,0:T(8,128)(2,1)S(1)}, u32[]{:S(2)}, u32[]{:S(2)}) collective-permute-start(bf16[64,2176]{1,0:T(8,128)(2,1)S(1)} %collective-permute-done.9), channel_id=1, source_target_pairs={{0,4},{2,6},{8,0},{10,2},{16,8},{18,10},{24,16},{26,18},{28,24},{3... | collective-permute-start | bytes 835592 | tf_op jit(solution)/shard_map/ppermute | solution.py:257
  91.0 28.0 %collective-permute-start.19 = (bf16[576,1024]{1,0:T(8,128)(2,1)S(1)}, bf16[576,1024]{1,0:T(8,128)(2,1)S(1)}, u32[]{:S(2)}, u32[]{:S(2)}) collective-permute-start(bf16[576,1024]{1,0:T(8,128)(2,1)S(1)} %copy-done.9), channel_id=1, source_target_pairs={{0,1},{1,0},{2,3},{3,2},{4,5},{5,4},{6,7},{7,6},{8,9},{9,8},{10,11... | collective-permute-start | bytes 3538952 | tf_op jit(solution)/shard_map/ppermute | solution.py:321
  213.4 27.5 %collective-permute-start.21 = (bf16[576,1024]{1,0:T(8,128)(2,1)}, bf16[576,1024]{1,0:T(8,128)(2,1)}, u32[]{:S(2)}, u32[]{:S(2)}) collective-permute-start(bf16[576,1024]{1,0:T(8,128)(2,1)} %get-tuple-element.89), channel_id=1, source_target_pairs={{0,1},{1,0},{2,3},{3,2},{4,5},{5,4},{6,7},{7,6},{8,9},{9,8},{10,11... | collective-permute-start | bytes 3538952 | tf_op jit(solution)/shard_map/ppermute | solution.py:321
  221.8 47.4 %collective-permute-start.32 = (bf16[8,64,2048]{2,1,0:T(8,128)(2,1)}, bf16[8,64,2048]{2,1,0:T(8,128)(2,1)}, u32[]{:S(2)}, u32[]{:S(2)}) collective-permute-start(bf16[8,64,2048]{2,1,0:T(8,128)(2,1)} %dynamic-slice_bitcast_fusion.1), channel_id=1, source_target_pairs={{0,2},{2,0},{4,6},{6,4},{8,10},{10,8},{12,14},{14,12},{16,18},{18,... | collective-permute-start | bytes 6291464 | tf_op jit(solution)/shard_map/ppermute | solution.py:260
  259.0 26.2 %collective-permute-start.20 = (bf16[576,1024]{1,0:T(8,128)(2,1)}, bf16[576,1024]{1,0:T(8,128)(2,1)S(1)}, u32[]{:S(2)}, u32[]{:S(2)}) collective-permute-start(bf16[576,1024]{1,0:T(8,128)(2,1)} %add_convert_fusion.4), channel_id=1, source_target_pairs={{0,1},{1,0},{2,3},{3,2},{4,5},{5,4},{6,7},{7,6},{8,9},{9,8},{10,11... | collective-permute-start | bytes 3538952 | tf_op jit(solution)/shard_map/ppermute | solution.py:321
  263.6 27.2 %collective-permute-start.23 = (bf16[8,64,2176]{2,1,0:T(8,128)(2,1)S(1)}, bf16[8,64,2176]{2,1,0:T(8,128)(2,1)S(1)}, u32[]{:S(2)}, u32[]{:S(2)}) collective-permute-start(bf16[8,64,2176]{2,1,0:T(8,128)(2,1)S(1)} %dynamic-slice_bitcast_fusion), channel_id=1, source_target_pairs={{0,2},{2,0},{4,6},{6,4},{8,10},{10,8},{12,14},{14,12},{16,18},{18,... | collective-permute-start | bytes 6684680 | tf_op jit(solution)/shard_map/ppermute | solution.py:260
  270.4 18.3 %collective-permute-start.33 = (bf16[32,2048]{1,0:T(8,128)(2,1)S(1)}, bf16[32,2048]{1,0:T(8,128)(2,1)S(1)}, u32[]{:S(2)}, u32[]{:S(2)}) collective-permute-start(bf16[32,2048]{1,0:T(8,128)(2,1)S(1)} %get-tuple-element.79), channel_id=1, source_target_pairs={{0,8},{2,10},{8,16},{10,18},{16,24},{18,26},{24,28},{26,30},{28,20... | collective-permute-start | bytes 393224 | tf_op jit(solution)/shard_map/ppermute | solution.py:254
  288.6 38.5 %collective-permute-start.37 = (bf16[32,2048]{1,0:T(8,128)(2,1)S(1)}, bf16[32,2048]{1,0:T(8,128)(2,1)S(1)}, u32[]{:S(2)}, u32[]{:S(2)}) collective-permute-start(bf16[32,2048]{1,0:T(8,128)(2,1)S(1)} %get-tuple-element.80), channel_id=1, source_target_pairs={{0,4},{2,6},{8,0},{10,2},{16,8},{18,10},{24,16},{26,18},{28,24},{3... | collective-permute-start | bytes 393224 | tf_op jit(solution)/shard_map/ppermute | solution.py:257
  288.8 14.6 %collective-permute-start.34 = (bf16[64,2048]{1,0:T(8,128)(2,1)S(1)}, bf16[64,2048]{1,0:T(8,128)(2,1)S(1)}, u32[]{:S(2)}, u32[]{:S(2)}) collective-permute-start(bf16[64,2048]{1,0:T(8,128)(2,1)S(1)} %pad_maximum_fusion.6), channel_id=1, source_target_pairs={{0,8},{2,10},{8,16},{10,18},{16,24},{18,26},{24,28},{26,30},{28,20... | collective-permute-start | bytes 786440 | tf_op jit(solution)/shard_map/ppermute | solution.py:254
  291.0 18.4 %collective-permute-start.24 = (bf16[32,2176]{1,0:T(8,128)(2,1)S(1)}, bf16[32,2176]{1,0:T(8,128)(2,1)S(1)}, u32[]{:S(2)}, u32[]{:S(2)}) collective-permute-start(bf16[32,2176]{1,0:T(8,128)(2,1)S(1)} %get-tuple-element.77), channel_id=1, source_target_pairs={{0,8},{2,10},{8,16},{10,18},{16,24},{18,26},{24,28},{26,30},{28,20... | collective-permute-start | bytes 417800 | tf_op jit(solution)/shard_map/ppermute | solution.py:254
  309.4 14.3 %collective-permute-start.25 = (bf16[64,2176]{1,0:T(8,128)(2,1)S(1)}, bf16[64,2176]{1,0:T(8,128)(2,1)S(1)}, u32[]{:S(2)}, u32[]{:S(2)}) collective-permute-start(bf16[64,2176]{1,0:T(8,128)(2,1)S(1)} %pad_maximum_fusion.4), channel_id=1, source_target_pairs={{0,8},{2,10},{8,16},{10,18},{16,24},{18,26},{24,28},{26,30},{28,20... | collective-permute-start | bytes 835592 | tf_op jit(solution)/shard_map/ppermute | solution.py:254
  327.3 16.9 %collective-permute-start.38 = (bf16[64,2048]{1,0:T(8,128)(2,1)S(1)}, bf16[64,2048]{1,0:T(8,128)(2,1)S(1)}, u32[]{:S(2)}, u32[]{:S(2)}) collective-permute-start(bf16[64,2048]{1,0:T(8,128)(2,1)S(1)} %pad_maximum_fusion.7), channel_id=1, source_target_pairs={{0,4},{2,6},{8,0},{10,2},{16,8},{18,10},{24,16},{26,18},{28,24},{3... | collective-permute-start | bytes 786440 | tf_op jit(solution)/shard_map/ppermute | solution.py:257
  328.6 39.2 %collective-permute-start.36 = (bf16[64,2048]{1,0:T(8,128)(2,1)S(1)}, bf16[64,2048]{1,0:T(8,128)(2,1)S(1)}, u32[]{:S(2)}, u32[]{:S(2)}) collective-permute-start(bf16[64,2048]{1,0:T(8,128)(2,1)S(1)} %get-tuple-element.65), channel_id=1, source_target_pairs={{0,8},{2,10},{8,16},{10,18},{16,24},{18,26},{24,28},{26,30},{28,20... | collective-permute-start | bytes 786440 | tf_op jit(solution)/shard_map/ppermute | solution.py:254
  345.2 15.7 %collective-permute-start.39 = (bf16[64,2048]{1,0:T(8,128)(2,1)S(1)}, bf16[64,2048]{1,0:T(8,128)(2,1)S(1)}, u32[]{:S(2)}, u32[]{:S(2)}) collective-permute-start(bf16[64,2048]{1,0:T(8,128)(2,1)S(1)} %fusion.51), channel_id=1, source_target_pairs={{0,4},{2,6},{8,0},{10,2},{16,8},{18,10},{24,16},{26,18},{28,24},{3... | collective-permute-start | bytes 786440 | tf_op jit(solution)/shard_map/ppermute | solution.py:257
  (86 other events, 889.8 us)
Sparse Core Ops, SparseCore 0:
  13.5 88.2 all-gather.1
  259.6 92.9 reduce-scatter.1
